TPU v7x, 32 devices: a whole 2x2x4 slice. The times are simulated.
32 devices in a mesh: rep: 8 (over y, x, core), shard: 4 (over z).
Axes of the slice: x: 2, y: 2, z: 4, core: 2. Of those that a mesh axis runs over, the one named last changes fastest.
Arguments:
- tokens: bfloat16 [16384, 1024], P(('rep', 'shard')), may hold values from -6 to 6
- doc_ids: int32 [16384], P(('rep', 'shard')), may hold values from 0 to 511, as said below
- routes: int32 [16384, 8], P(('rep', 'shard')), may hold values from 0 to 15, all different within a row; in each aligned block of 512 rows (0 to 511, 512 to 1023, ...) at most 288 rows name the same one
- norm_in_gain: bfloat16 [1024], P('shard'), may hold values from 0.5 to 1.5
- w_query: bfloat16 [1024, 1024], P('shard'), may hold values from -0.1875 to 0.1875
- w_key: bfloat16 [1024, 512], P('shard'), may hold values from -0.1875 to 0.1875
- w_value: bfloat16 [1024, 512], P('shard'), may hold values from -0.1875 to 0.1875
- w_out: bfloat16 [1024, 1024], P('shard'), may hold values from -0.75 to 0.75
- norm_mid_gain: bfloat16 [1024], P('shard'), may hold values from 0.5 to 1.5
- w_router: bfloat16 [1024, 16], P('shard'), may hold values from -0.09375 to 0.09375
- w_expert_in: bfloat16 [16, 1024, 1024], P('shard'), may hold values from -0.1875 to 0.1875
- w_expert_down: bfloat16 [16, 512, 1024], P('shard'), may hold values from -0.75 to 0.75
- cotangent: bfloat16 [16384, 1024], P(('rep', 'shard')), may hold values from -6 to 6
Outputs:
- mixed: bfloat16 [16384, 1024], P(('rep', 'shard'))
- grad_tokens: float32 [16384, 1024], P(('rep', 'shard'))
- grad_norm_in_gain: float32 [1024], P('shard')
- grad_w_query: float32 [1024, 1024], P('shard')
- grad_w_key: float32 [1024, 512], P('shard')
- grad_w_value: float32 [1024, 512], P('shard')
- grad_w_out: float32 [1024, 1024], P('shard')
- grad_norm_mid_gain: float32 [1024], P('shard')
- grad_w_router: float32 [1024, 16], P('shard')
- grad_w_expert_in: float32 [16, 1024, 1024], P('shard')
- grad_w_expert_down: float32 [16, 512, 1024], P('shard')
Inputs may be any that keep to these rules, and one draw needn't show every extreme that they name: `doc_ids`: in every aligned block of 512 tokens the numbers start at 0 and rise by 0 or 1 from token to token. Among the 512 tokens of one device, no expert is named by more than 288 routes.
All inputs are finite; a program needn't handle non-finite values.
Results may differ from a plain program's by a relative error of at most 0.019.
Values may be sent and summed in bfloat16 or wider, within the bound.
A program may use at most 320 MiB of HBM per device.

v0:
```python
import jax
import jax.numpy as jnp
from jax import lax
from jax.sharding import PartitionSpec as P

HEADS = 16
KV_HEADS = 8
HEAD_DIM = 64
EXPERTS = 16
PAD = 128
epsilon = 1e-06
rope_base = 10000.0
masked_score = -1e30


def positions(doc_rows):
    row_count = doc_rows.shape[0]
    places = jnp.arange(row_count, dtype=jnp.int32)
    opening = jnp.concatenate([jnp.ones((1,), dtype=jnp.bool_), doc_rows[1:] != doc_rows[:-1]])
    begins = lax.cummax(jnp.where(opening, places, 0), axis=0)
    return places - begins


def rotary_tables(places, head_width):
    half_width = head_width // 2
    frequencies = jnp.power(
        rope_base, -2.0 * jnp.arange(half_width, dtype=jnp.float32) / head_width
    )
    angles = places.astype(jnp.float32)[:, None] * frequencies[None, :]
    return (jnp.cos(angles)[:, None, :], jnp.sin(angles)[:, None, :])


def rotate(values, cosine, sine_table):
    half_width = values.shape[-1] // 2
    former, latter = (values[..., :half_width], values[..., half_width:])
    return jnp.concatenate(
        [former * cosine - latter * sine_table, latter * cosine + former * sine_table], axis=-1
    )


def unrotate(values, cosine, sine_table):
    half_width = values.shape[-1] // 2
    former, latter = (values[..., :half_width], values[..., half_width:])
    return jnp.concatenate(
        [former * cosine + latter * sine_table, latter * cosine - former * sine_table], axis=-1
    )


def normalize(values):
    row_scale = lax.rsqrt(jnp.mean(values * values, axis=-1, keepdims=True) + epsilon)
    return (values * row_scale, row_scale)


def norm_back(grad_scaled, normed, row_scale, gain_full):
    grad_normed = grad_scaled * gain_full
    inner = jnp.mean(grad_normed * normed, axis=-1, keepdims=True)
    return (row_scale * (grad_normed - normed * inner), jnp.sum(grad_scaled * normed, axis=0))


def score_block(query_blk, key_part, doc_query, doc_key):
    scores = jnp.einsum(
        "qgrd,kgd->grqk", query_blk, key_part, preferred_element_type=jnp.float32
    ) * query_blk.shape[-1] ** (-0.5)
    query_place = jnp.arange(query_blk.shape[0], dtype=jnp.int32)
    key_place = jnp.arange(key_part.shape[0], dtype=jnp.int32)
    allowed = (doc_query[:, None] == doc_key[None, :]) & (
        query_place[:, None] >= key_place[None, :]
    )
    return jnp.where(allowed, scores, masked_score)


def attend(query_rows, key_rows, value_rows, doc_rows):
    scores = score_block(query_rows, key_rows, doc_rows, doc_rows)
    row_max = jnp.max(scores, axis=-1, keepdims=True)
    exponent = jnp.exp(scores - row_max)
    row_total = jnp.sum(exponent, axis=-1, keepdims=True)
    probs_low = (exponent / row_total).astype(jnp.bfloat16)
    outputs = jnp.einsum(
        "grqk,kgd->qgrd", probs_low, value_rows, preferred_element_type=jnp.float32
    ).astype(jnp.bfloat16)
    lse_parts = row_max + jnp.log(row_total)
    return (outputs, lse_parts)


def attend_back(query_rows, key_rows, value_rows, doc_rows, log_sums, grad_att):
    row_count = query_rows.shape[0]
    block_rows = min(512, row_count)
    scale_factor = query_rows.shape[-1] ** (-0.5)
    grad_key = jnp.zeros(key_rows.shape, jnp.float32)
    grad_value = jnp.zeros(value_rows.shape, jnp.float32)
    scores = score_block(query_rows, key_rows, doc_rows, doc_rows)
    probs = jnp.exp(scores - log_sums)
    grad_probs = jnp.einsum(
        "qgrd,kgd->grqk", grad_att, value_rows, preferred_element_type=jnp.float32
    )
    inner = jnp.sum(probs * grad_probs, axis=-1, keepdims=True)
    grad_scores = (probs * (grad_probs - inner)).astype(jnp.bfloat16)
    query_parts = (
        jnp.einsum("grqk,kgd->qgrd", grad_scores, key_rows, preferred_element_type=jnp.float32)
        * scale_factor
    )
    grad_key = grad_key.at[:block_rows].add(
        jnp.einsum("grqk,qgrd->kgd", grad_scores, query_rows, preferred_element_type=jnp.float32)
        * scale_factor
    )
    grad_value = grad_value.at[:block_rows].add(
        jnp.einsum(
            "grqk,qgrd->kgd",
            probs.astype(jnp.bfloat16),
            grad_att,
            preferred_element_type=jnp.float32,
        )
    )
    return (query_parts, grad_key, grad_value)


def gather_shard(piece):
    return lax.all_gather(piece, "shard", axis=0, tiled=True)


def shards(
    tokens,
    doc_ids,
    routes,
    norm_in_gain,
    w_query,
    w_key,
    w_value,
    w_out,
    norm_mid_gain,
    w_router,
    w_expert_in,
    w_expert_down,
    cotangent,
):
    bf16, f32 = (jnp.bfloat16, jnp.float32)
    row_count, model_width = tokens.shape
    groups = HEADS // KV_HEADS
    query_cols = w_query.shape[1]
    kv_cols = w_key.shape[1]
    own_rows = w_query.shape[0]
    own_experts, ff = w_expert_down.shape[:2]
    shard_at = lax.axis_index("shard")
    small = jnp.concatenate(
        [
            w_router,
            norm_in_gain[:, None],
            norm_mid_gain[:, None],
            jnp.zeros((own_rows, PAD - EXPERTS - 2), bf16),
        ],
        axis=1,
    )
    qkv_full = gather_shard(jnp.concatenate([w_query, w_key, w_value, small], axis=1))
    qkv_w = qkv_full[:, : query_cols + 2 * kv_cols]
    small_full = qkv_full[:, query_cols + 2 * kv_cols :]
    router_full = small_full[:, :EXPERTS]
    gain_in = small_full[:, EXPERTS].astype(f32)
    gain_mid = small_full[:, EXPERTS + 1].astype(f32)
    out_w = gather_shard(w_out)
    mask_own = jnp.any(
        routes[:, :, None] == jnp.arange(EXPERTS, dtype=jnp.int32)[None, None, :], axis=1
    )
    side = jnp.concatenate(
        [cotangent, mask_own.astype(bf16), jnp.zeros((row_count, PAD - EXPERTS), bf16)], axis=1
    )
    side_all = gather_shard(side)
    dy_all = side_all[:, :model_width]
    mask_all = side_all[:, model_width : model_width + EXPERTS] > 0
    inputs = tokens.astype(f32)
    grad_final = cotangent.astype(f32)
    cosine, sine_table = rotary_tables(positions(doc_ids), HEAD_DIM)
    normed_in, scale_in = normalize(inputs)
    first_low = (normed_in * gain_in).astype(bf16)
    qkv_pre = jnp.dot(first_low, qkv_w, preferred_element_type=f32)
    query_pre = qkv_pre[:, :query_cols]
    key_pre = qkv_pre[:, query_cols : query_cols + kv_cols]
    value_pre = qkv_pre[:, query_cols + kv_cols :]
    query_rows = (
        rotate(query_pre.reshape(row_count, HEADS, HEAD_DIM), cosine, sine_table)
        .astype(bf16)
        .reshape(row_count, KV_HEADS, groups, HEAD_DIM)
    )
    key_rows = rotate(key_pre.reshape(row_count, KV_HEADS, HEAD_DIM), cosine, sine_table).astype(
        bf16
    )
    value_rows = value_pre.astype(bf16).reshape(row_count, KV_HEADS, HEAD_DIM)
    att_rows, log_sums = attend(query_rows, key_rows, value_rows, doc_ids)
    att_low = att_rows.reshape(row_count, query_cols)
    middle = inputs + jnp.dot(att_low, out_w, preferred_element_type=f32)
    normed_mid, scale_mid = normalize(middle)
    second_low = (normed_mid * gain_mid).astype(bf16)
    second_all = gather_shard(second_low)
    logits = jnp.dot(second_all, router_full, preferred_element_type=f32)
    chosen = jnp.where(mask_all, logits, masked_score)
    gate_exp = jnp.where(mask_all, jnp.exp(chosen - jnp.max(chosen, axis=1, keepdims=True)), 0.0)
    gates_all = gate_exp / jnp.sum(gate_exp, axis=1, keepdims=True)
    gates_here = lax.dynamic_slice_in_dim(gates_all, shard_at * own_experts, own_experts, axis=1)
    gates_own = lax.dynamic_slice_in_dim(gates_all, shard_at * row_count, row_count, axis=0)
    gated, grad_both, grad_gates_here = experts(
        second_all, dy_all, gates_here, w_expert_in, w_expert_down
    )
    combined = jnp.einsum("etf,efd->td", gated, w_expert_down, preferred_element_type=f32)
    combined_own = lax.psum_scatter(combined.astype(bf16), "shard", scatter_dimension=0, tiled=True)
    grad_second_here = jnp.einsum("etf,edf->td", grad_both, w_expert_in, preferred_element_type=f32)
    gate_cols = lax.dynamic_update_slice_in_dim(
        jnp.zeros((grad_gates_here.shape[0], EXPERTS), f32),
        grad_gates_here,
        shard_at * own_experts,
        axis=1,
    )
    gate_high = gate_cols.astype(bf16)
    gate_low = (gate_cols - gate_high.astype(f32)).astype(bf16)
    back_rows = jnp.concatenate(
        [
            grad_second_here.astype(bf16),
            gate_high,
            gate_low,
            jnp.zeros((gate_cols.shape[0], PAD - 2 * EXPERTS), bf16),
        ],
        axis=1,
    )
    back_own = lax.psum_scatter(back_rows, "shard", scatter_dimension=0, tiled=True)
    grad_in_here = jnp.einsum("td,etf->edf", second_all, grad_both, preferred_element_type=f32)
    grad_down_here = jnp.einsum("etf,td->efd", gated, dy_all, preferred_element_type=f32)
    grad_in_own = lax.psum(grad_in_here.astype(bf16), "rep").astype(f32)
    grad_down_own = lax.psum(grad_down_here.astype(bf16), "rep").astype(f32)
    mixed = (middle + combined_own.astype(f32)).astype(bf16)
    gate_back = back_own[:, model_width : model_width + 2 * EXPERTS].astype(f32)
    grad_gates = gate_back[:, :EXPERTS] + gate_back[:, EXPERTS:]
    grad_logits = (
        gates_own * (grad_gates - jnp.sum(gates_own * grad_gates, axis=1, keepdims=True))
    ).astype(bf16)
    grad_router = jnp.einsum("td,te->de", second_low, grad_logits, preferred_element_type=f32)
    grad_second = back_own[:, :model_width].astype(f32) + jnp.einsum(
        "te,de->td", grad_logits, router_full, preferred_element_type=f32
    )
    grad_mid_norm, grad_gain_mid = norm_back(grad_second, normed_mid, scale_mid, gain_mid)
    grad_middle = grad_final + grad_mid_norm
    grad_branch = grad_middle.astype(bf16)
    grad_out_w = jnp.einsum("ta,td->ad", att_low, grad_branch, preferred_element_type=f32)
    grad_att = jnp.einsum("td,ad->ta", grad_branch, out_w, preferred_element_type=f32).astype(bf16)
    grad_query_rot, grad_key_rot, grad_value_rows = attend_back(
        query_rows,
        key_rows,
        value_rows,
        doc_ids,
        log_sums,
        grad_att.reshape(row_count, KV_HEADS, groups, HEAD_DIM),
    )
    grad_query_pre = (
        unrotate(grad_query_rot.reshape(row_count, HEADS, HEAD_DIM), cosine, sine_table)
        .astype(bf16)
        .reshape(row_count, query_cols)
    )
    grad_key_pre = unrotate(grad_key_rot, cosine, sine_table).astype(bf16)
    grad_pre = jnp.concatenate(
        [
            grad_query_pre,
            grad_key_pre.reshape(row_count, kv_cols),
            grad_value_rows.astype(bf16).reshape(row_count, kv_cols),
        ],
        axis=1,
    )
    grad_qkv = jnp.einsum("td,tc->dc", first_low, grad_pre, preferred_element_type=f32)
    columns = jnp.einsum("tc,dc->td", grad_pre, qkv_w, preferred_element_type=f32)
    grad_in_norm, grad_gain_in = norm_back(columns, normed_in, scale_in, gain_in)
    grad_tokens = grad_middle + grad_in_norm
    joint = jnp.concatenate(
        [
            grad_qkv.astype(bf16),
            grad_out_w.astype(bf16),
            grad_router.astype(bf16),
            grad_gain_in.astype(bf16)[:, None],
            grad_gain_mid.astype(bf16)[:, None],
            jnp.zeros((model_width, PAD - EXPERTS - 2), bf16),
        ],
        axis=1,
    )
    joint_own = reduce_joint(joint).astype(f32)
    edges = [0]
    for width in (query_cols, kv_cols, kv_cols, w_out.shape[1], EXPERTS, 1, 1):
        edges.append(edges[-1] + width)
    pieces = [joint_own[:, a:b] for a, b in zip(edges[:-1], edges[1:])]
    query_own, key_own, value_own, out_own, router_own, gain_in_own, gain_mid_own = pieces
    return (
        mixed,
        grad_tokens,
        gain_in_own[:, 0],
        query_own,
        key_own,
        value_own,
        out_own,
        gain_mid_own[:, 0],
        router_own,
        grad_in_own,
        grad_down_own,
    )


def reduce_joint(joint):
    part = lax.psum_scatter(joint, "shard", scatter_dimension=0, tiled=True)
    return lax.psum(part, "rep")


def experts(rows, dy_rows, gates, in_w, down_w):
    f32, bf16 = (jnp.float32, jnp.bfloat16)
    both = jnp.einsum("td,edf->etf", rows, in_w, preferred_element_type=f32)
    half_width = both.shape[-1] // 2
    gate_part, up_part = (both[..., :half_width], both[..., half_width:])
    sigmoid_gate = jax.nn.sigmoid(gate_part)
    silu_gate = gate_part * sigmoid_gate
    hidden = (silu_gate * up_part).astype(bf16).astype(f32)
    back = jnp.einsum("td,efd->etf", dy_rows, down_w, preferred_element_type=f32)
    gate_cols = gates.T[:, :, None]
    grad_gates = jnp.sum(hidden * back, axis=-1).T
    gated = (hidden * gate_cols).astype(bf16)
    grad_hidden = back * gate_cols
    grad_gate = grad_hidden * up_part * sigmoid_gate * (1.0 + gate_part * (1.0 - sigmoid_gate))
    grad_both = jnp.concatenate([grad_gate, grad_hidden * silu_gate], axis=-1).astype(bf16)
    return (gated, grad_both, grad_gates)


def solution(mesh):
    in_specs = (
        P(("rep", "shard"), None),
        P(("rep", "shard")),
        P(("rep", "shard"), None),
        P("shard"),
        P("shard", None),
        P("shard", None),
        P("shard", None),
        P("shard", None),
        P("shard"),
        P("shard", None),
        P("shard", None, None),
        P("shard", None, None),
        P(("rep", "shard"), None),
    )
    out_specs = (
        P(("rep", "shard"), None),
        P(("rep", "shard"), None),
        P("shard"),
        P("shard", None),
        P("shard", None),
        P("shard", None),
        P("shard", None),
        P("shard"),
        P("shard", None),
        P("shard", None, None),
        P("shard", None, None),
    )
    return jax.shard_map(shards, mesh=mesh, in_specs=in_specs, out_specs=out_specs, check_vma=False)
```

profile of v0, /device:TPU:0, one launch (start us, length us, event | category | flops | bytes accessed | tf_op | source)
XLA Modules:
  0.0 990.5 jit_solution(4883131591927317545)
XLA Ops:
  18.9 81.9 %all-gather.5.cloned.1.call-done = bf16[1024,2176]{1,0:T(8,128)(2,1)} async-done(((bf16[256,2176]{1,0:T(8,128)(2,1)}), bf16[1024,2176]{1,0:T(8,128)(2,1)}) %all-gather.5.cloned.1.call-update) | async-done | bytes 4456464 | tf_op jit(solution)/shard_map/all_gather | solution.py:118
  118.9 7.7 fusion.70
  126.6 8.3 fusion.6
  135.6 8.7 fusion.41
  151.5 85.6 %all-gather.11.cloned.1.call-done = bf16[2048,1152]{0,1:T(8,128)(2,1)} async-done(((bf16[512,1152]{0,1:T(8,128)(2,1)}), bf16[2048,1152]{0,1:T(8,128)(2,1)}) %all-gather.11.cloned.1.call-update) | async-done | bytes 4718608 | tf_op jit(solution)/shard_map/all_gather | solution.py:118
  237.1 81.2 %all-gather.9.cloned.1.call-done = bf16[2048,1024]{0,1:T(8,128)(2,1)} async-done(((bf16[512,1024]{0,1:T(8,128)(2,1)}), bf16[2048,1024]{0,1:T(8,128)(2,1)}) %all-gather.9.cloned.1.call-update) | async-done | bytes 4194320 | tf_op jit(solution)/shard_map/all_gather | solution.py:118
  323.3 23.1 %convolution_bitcast_fusion = f32[4,2048,1024]{1,2,0:T(8,128)} fusion(bf16[4,1024,1024]{2,1,0:T(8,128)(2,1)} %param.31, bf16[2048,1024]{0,1:T(8,128)(2,1)S(1)} %copy-done.9), kind=kOutput, calls=%fused_computation.2 | convolution fusion | flops 17179869184 | bytes 46137344 | tf_op jit(solution)/shard_map/td,edf->etf/dot_general | solution.py:307
  346.4 28.4 %multiply_convert_fusion.1 = (bf16[4,2048,512]{1,2,0:T(8,128)(2,1)}, bf16[4,2048,512]{1,2,0:T(8,128)(2,1)}, f32[4,2048]{1,0:T(4,128)S(1)}, bf16[4,2048,512]{1,2,0:T(8,128)(2,1)}) fusion(f32[4,2048,1024]{1,2,0:T(8,128)} %convolution_bitcast_fusion, f32[4,2048]{1,0:T(4,128)S(1)} %dynamic-slice_bitcast_fusion, bf16[4,512,1024]{2,1,0:T(8,128)(2,1)} %param.32, ...), kind=kOutput, calls=%fused_computation.15 | convolution fusion | flops 8669618176 | bytes 67174400 | tf_op jit(solution)/shard_map/td,efd->etf/dot_general | solution.py:313
  374.8 22.7 %bitcast_convert_fusion = bf16[2048,1024]{0,1:T(8,128)(2,1)S(1)} fusion(bf16[4,1024,1024]{2,1,0:T(8,128)(2,1)} %param.31, bf16[4,2048,512]{1,2,0:T(8,128)(2,1)} %get-tuple-element.122, bf16[4,2048,512]{1,2,0:T(8,128)(2,1)} %get-tuple-element.121), kind=kOutput, calls=%fused_computation.26 | convolution fusion | flops 17215520768 | bytes 29360128 | tf_op jit(solution)/shard_map/etf,edf->td/dot_general | solution.py:204
  397.6 6.7 maximum_maximum_fusion
  404.4 14.1 %bitcast_convert_fusion.1 = bf16[2048,1024]{0,1:T(8,128)(2,1)} fusion(bf16[4,512,1024]{2,1,0:T(8,128)(2,1)} %param.32, bf16[4,2048,512]{1,2,0:T(8,128)(2,1)} %get-tuple-element.124, f32[4,2048]{1,0:T(4,128)S(1)} %dynamic-slice_bitcast_fusion), kind=kOutput, calls=%fused_computation.27 | convolution fusion | flops 8604614656 | bytes 16809984 | tf_op jit(solution)/shard_map/etf,efd->td/dot_general | solution.py:202
  419.9 68.4 %reduce-scatter.6.cloned.1.call-done = bf16[512,1152]{0,1:T(8,128)(2,1)} async-done(((bf16[2048,1152]{0,1:T(8,128)(2,1)}), bf16[512,1152]{0,1:T(8,128)(2,1)}) %reduce-scatter.6.cloned.1.call-update) | async-done | bytes 1179664 | tf_op jit(solution)/shard_map/reduce_scatter | solution.py:222
  492.4 75.3 %reduce-scatter.4.cloned.1.call-done = bf16[512,1024]{0,1:T(8,128)(2,1)} async-done(((bf16[2048,1024]{0,1:T(8,128)(2,1)}), bf16[512,1024]{0,1:T(8,128)(2,1)}) %reduce-scatter.4.cloned.1.call-update) | async-done | bytes 1048592 | tf_op jit(solution)/shard_map/reduce_scatter | solution.py:203
  574.8 15.1 %fusion.2 = (f32[8,2,512]{2,1,0:T(2,128)S(1)}, f32[8,512,512,2]{2,1,3,0:T(8,128)}) fusion(f32[8,2,512,512]{2,3,1,0:T(8,128)} %get-tuple-element.142, f32[8,2,512]{2,1,0:T(2,128)} %bitcast.136, bf16[512,8,64,1]{0,2,3,1:T(8,128)(2,1)S(1)} %bitcast.125, bf16[512,8,2,64]{0,3,2,1:T(8,128)(2,1)S(1)} %bitcast.119), kind=kOutput, calls=%fused_computation.8 | convolution fusion | flops 549445632 | bytes 35192832 | tf_op jit(solution)/shard_map/qgrd,kgd->grqk/dot_general | solution.py:93
  591.2 8.3 fusion.4
  605.8 6.0 fusion.46
  626.9 5.0 fusion.39
  634.6 10.6 %concatenate.62 = bf16[1024,3200]{1,0:T(8,128)(2,1)} concatenate(bf16[1024,2048]{1,0:T(8,128)(2,1)} %convolution_convert_fusion, bf16[1024,1024]{1,0:T(8,128)(2,1)S(1)} %copy-done.17, bf16[1024,16]{1,0:T(8,128)(2,1)} %copy.153, bf16[1024,1]{1,0:T(8,128)(2,1)S(1)} %convert_element_type.230, bf16[1024,1]{1,0:T(8,128)(2,1)} %convert_element_type.231, bf16[1024,110]{1,0:T(8,128)(2,1)} %broadcast_in_dim.43), dimensions={1} | concatenate | bytes 13107200 | tf_op jit(solution)/shard_map/concatenate | solution.py:268
  646.0 13.8 %fusion.31 = bf16[4,512,1024]{2,1,0:T(8,128)(2,1)} fusion(bf16[2048,1152]{0,1:T(8,128)(2,1)} %all-gather.11.cloned.1.call-done, bf16[4,2048,512]{1,2,0:T(8,128)(2,1)} %get-tuple-element.124, f32[4,2048]{1,0:T(4,128)S(1)} %copy-done.36), kind=kOutput, calls=%fused_computation.50 | convolution fusion | flops 8604614656 | bytes 16809984 | tf_op jit(solution)/shard_map/etf,td->efd/dot_general | solution.py:224
  659.8 24.8 %convert_bitcast_fusion = bf16[4,1024,1024]{1,2,0:T(8,128)(2,1)} fusion(bf16[4,2048,512]{1,2,0:T(8,128)(2,1)} %get-tuple-element.122, bf16[4,2048,512]{1,2,0:T(8,128)(2,1)} %get-tuple-element.121, bf16[2048,1024]{0,1:T(8,128)(2,1)} %all-gather.9.cloned.1.call-done), kind=kOutput, calls=%fused_computation.28 | convolution fusion | flops 17217617920 | bytes 29360128 | tf_op jit(solution)/shard_map/td,etf->edf/dot_general | solution.py:223
  684.6 76.3 %reduce-scatter.8.cloned.1.call-done = bf16[256,3200]{1,0:T(8,128)(2,1)} async-done(((bf16[1024,3200]{1,0:T(8,128)(2,1)}), bf16[256,3200]{1,0:T(8,128)(2,1)}) %reduce-scatter.8.cloned.1.call-update) | async-done | bytes 1638416 | tf_op jit(solution)/shard_map/reduce_scatter | solution.py:301
  766.8 191.1 %all-reduce.3.cloned.1.call-done = (bf16[4,1024,1024]{1,2,0:T(8,128)(2,1)}, bf16[256,3200]{1,0:T(8,128)(2,1)}, bf16[4,512,1024]{2,1,0:T(8,128)(2,1)}) async-done(((bf16[4,1024,1024]{1,2,0:T(8,128)(2,1)}, bf16[256,3200]{1,0:T(8,128)(2,1)}, bf16[4,512,1024]{2,1,0:T(8,128)(2,1)}), (bf16[4,1024,1024]{1,2,0:T(8,128)(2,1)}, bf16[256,3200]{1,0:T(8,128)(2,1)}, ...) | async-done | bytes 14221328 | tf_op jit(solution)/shard_map/psum | solution.py:225
  962.6 12.5 %copy.161 = f32[4,1024,1024]{2,1,0:T(8,128)} copy(bf16[4,1024,1024]{1,2,0:T(8,128)(2,1)} %get-tuple-element.114) | data formatting | bytes 25165824
  975.1 6.6 convert_element_type.227
  (195 shorter events, 92.8 us)
Async XLA Ops:
  7.2 93.6 %all-gather.5.cloned.1.call-start = ((), (), s32[]{:S(2)}) async-start(), calls=%async_computation.3 | async-start | bytes 5570560 | tf_op jit(solution)/shard_map/all_gather | solution.py:118
  12.8 134.0 %all-gather.7.cloned.1.call-start = ((), (), s32[]{:S(2)}) async-start(), calls=%async_computation.4 | async-start | bytes 2621440 | tf_op jit(solution)/shard_map/all_gather | solution.py:118
  13.6 223.5 %all-gather.11.cloned.1.call-start = ((), (), s32[]{:S(2)}) async-start(), calls=%async_computation.6 | async-start | bytes 5898240 | tf_op jit(solution)/shard_map/all_gather | solution.py:118
  14.2 92.8 %copy-start.5 = (bf16[512,1024]{0,1:T(8,128)(2,1)}, bf16[512,1024]{0,1:T(8,128)(2,1)S(1)}, u32[]{:S(2)}) copy-start(bf16[512,1024]{0,1:T(8,128)(2,1)S(1)} %copy.139) | copy-start | bytes 3145732
  15.7 302.6 %all-gather.9.cloned.1.call-start = ((), (), s32[]{:S(2)}) async-start(), calls=%async_computation.5 | async-start | bytes 5242880 | tf_op jit(solution)/shard_map/all_gather | solution.py:118
  17.3 129.5 %copy-start.3 = (bf16[512,1024]{0,1:T(8,128)(2,1)}, bf16[512,1024]{0,1:T(8,128)(2,1)S(1)}, u32[]{:S(2)}) copy-start(bf16[512,1024]{0,1:T(8,128)(2,1)S(1)} %copy.128) | copy-start | bytes 3145732
  18.3 88.8 %copy-start.40 = (f32[512]{0:T(512)}, f32[512]{0:T(512)S(1)}, u32[]{:S(2)}) copy-start(f32[512]{0:T(512)S(1)} %add_rsqrt_fusion.1) | copy-start | bytes 6148
  18.7 99.8 %copy-start.18 = (f32[512,32]{0,1:T(8,128)}, f32[512,32]{0,1:T(8,128)S(1)}, u32[]{:S(2)}) copy-start(f32[512,32]{0,1:T(8,128)S(1)} %get-tuple-element.139) | copy-start | bytes 196612
  18.7 99.8 %copy-start.20 = (f32[512,32]{0,1:T(8,128)}, f32[512,32]{0,1:T(8,128)S(1)}, u32[]{:S(2)}) copy-start(f32[512,32]{0,1:T(8,128)S(1)} %get-tuple-element.140) | copy-start | bytes 196612
  126.6 8.4 copy-start.29
  126.6 9.0 copy-start.11
  151.3 336.9 %reduce-scatter.6.cloned.1.call-start = ((), (), s32[]{:S(2)}) async-start(), calls=%async_computation.8 | async-start | bytes 5898240 | tf_op jit(solution)/shard_map/reduce_scatter | solution.py:222
  323.3 81.1 %copy-start.35 = (f32[4,2048]{1,0:T(4,128)}, f32[4,2048]{1,0:T(4,128)S(1)}, u32[]{:S(2)}) copy-start(f32[4,2048]{1,0:T(4,128)S(1)} %dynamic-slice_bitcast_fusion) | copy-start | bytes 98308
  404.3 163.4 %reduce-scatter.4.cloned.1.call-start = ((), (), s32[]{:S(2)}) async-start(), calls=%async_computation.7 | async-start | bytes 5242880 | tf_op jit(solution)/shard_map/reduce_scatter | solution.py:203
  418.5 149.3 %copy-start.6 = (bf16[512,1024]{0,1:T(8,128)(2,1)S(1)}, bf16[512,1024]{0,1:T(8,128)(2,1)}, u32[]{:S(2)}) copy-start(bf16[512,1024]{0,1:T(8,128)(2,1)} %copy-done.5) | copy-start | bytes 3145732
  418.5 342.5 %reduce-scatter.8.cloned.1.call-start = ((), (), s32[]{:S(2)}) async-start(), calls=%async_computation.9 | async-start | bytes 8192000 | tf_op jit(solution)/shard_map/reduce_scatter | solution.py:301
  574.7 15.1 %slice-start = ((s8[16777216]{0:T(1024)(128)(4,1)}), s8[4194304]{0:T(1024)(128)(4,1)S(1)}, s32[]{:S(2)}) async-start(s8[16777216]{0:T(1024)(128)(4,1)} %bitcast.117), calls=%async_computation.11 | async-start | bytes 8388608
  574.8 15.1 %slice-start.1 = ((s8[16777216]{0:T(1024)(128)(4,1)}), s8[4194304]{0:T(1024)(128)(4,1)S(1)}, s32[]{:S(2)}) async-start(s8[16777216]{0:T(1024)(128)(4,1)} %bitcast.117), calls=%async_computation.12 | async-start | bytes 8388608
  574.8 15.1 %slice-start.2 = ((s8[16777216]{0:T(1024)(128)(4,1)}), s8[4194304]{0:T(1024)(128)(4,1)S(1)}, s32[]{:S(2)}) async-start(s8[16777216]{0:T(1024)(128)(4,1)} %bitcast.117), calls=%async_computation.13 | async-start | bytes 8388608
  574.8 16.4 %slice-start.3 = ((s8[16777216]{0:T(1024)(128)(4,1)}), s8[4194304]{0:T(1024)(128)(4,1)S(1)}, s32[]{:S(2)}) async-start(s8[16777216]{0:T(1024)(128)(4,1)} %bitcast.117), calls=%async_computation.14 | async-start | bytes 8388608
  574.8 16.4 %copy-start.28 = (f32[2,8,512]{2,1,0:T(8,128)S(1)}, f32[2,8,512]{2,1,0:T(8,128)}, u32[]{:S(2)}) copy-start(f32[2,8,512]{2,1,0:T(8,128)} %log_add_fusion) | copy-start | bytes 98308
  591.2 11.7 %copy-start.24 = (bf16[512,8,32]{0,2,1:T(8,128)(2,1)S(1)}, bf16[512,8,32]{0,2,1:T(8,128)(2,1)}, u32[]{:S(2)}) copy-start(bf16[512,8,32]{0,2,1:T(8,128)(2,1)} %copy-done.23) | copy-start | bytes 786436
  591.2 11.7 %copy-start.26 = (bf16[512,8,32]{0,2,1:T(8,128)(2,1)S(1)}, bf16[512,8,32]{0,2,1:T(8,128)(2,1)}, u32[]{:S(2)}) copy-start(bf16[512,8,32]{0,2,1:T(8,128)(2,1)} %copy-done.25) | copy-start | bytes 786436
  645.3 312.7 %all-reduce.3.cloned.1.call-start = ((), (), s32[]{:S(2)}) async-start(), calls=%async_computation.10 | async-start | bytes 28442624 | tf_op jit(solution)/shard_map/psum | solution.py:225
  (33 other events, 138.8 us)
Sparse Core Ops, SparseCore 0:
  12.9 87.7 all-gather.4
  102.3 44.4 all-gather.6
  149.0 88.1 all-gather.10
  239.1 79.1 all-gather.8
  404.4 83.7 reduce-scatter.5
  490.4 77.2 reduce-scatter.3
  645.4 115.4 reduce-scatter.7
  766.1 191.8 all-reduce.2
where the time goes:
time: 1000 us; the launch traced here: 990 us
  waiting for transfers between devices  663 us (66%)
  matrix products  202 us (20%)
  local copies, waits for them, and re-layouts  60.7 us (6%)
  other arithmetic  49.2 us (5%)
  between operations  15.4 us (2%)
    all_gather x4, waiting for transfers between devices, gather_shard(): return lax.all_gather(piece, 'shard', axis=0, tiled=True)  251 us
    psum x1, waiting for transfers between devices, shards(): grad_in_own = lax.psum(grad_in_here.astype(bf16), 'rep').astype(f32)  191 us
    reduce_scatter x1, waiting for transfers between devices, reduce_joint(): part = lax.psum_scatter(joint, 'shard', scatter_dimension=0, tiled=True)  76.3 us
    reduce_scatter x1, waiting for transfers between devices, shards(): lax.psum_scatter(combined.astype(bf16), 'shard', scatter_dimension=0, til...  75.3 us
    reduce_scatter x1, waiting for transfers between devices, shards(): lax.psum_scatter(back_rows, 'shard', scatter_dimension=0, tiled=True)  68.4 us
    dot_general x1, matrix products, experts(): jnp.einsum('td,efd->etf', dy_rows, down_w, preferred_element_type=f32)  28.4 us
    unnamed x105, local copies, waits for them, and re-layouts  28 us
    dot_general x1, matrix products, shards(): jnp.einsum('td,etf->edf', second_all, grad_both, preferred_element_type=f32)  24.8 us
  transfers between devices with their start and end apart: 8, of which 8 were waited for; matrix products, arithmetic and copies ran while one was open for 12% of the time, Pallas kernels for 0%

commit v1 on v0

--- a/solution.py
+++ b/solution.py
@@ -11,6 +11,24 @@
 epsilon = 1e-06
 rope_base = 10000.0
 masked_score = -1e30
+
+
+def collect(array, axis, dim):
+    ways, here, hop = (lax.axis_size(axis), lax.axis_index(axis), array.shape[dim])
+    dims = [n * ways if d == dim else n for d, n in enumerate(array.shape)]
+    full = lax.dynamic_update_slice_in_dim(
+        jnp.zeros(dims, array.dtype), array, here * hop, axis=dim
+    )
+    going_up = going_down = array
+    for far in range(1, ways // 2 + 1):
+        going_up = lax.ppermute(going_up, axis, [(d, (d + 1) % ways) for d in range(ways)])
+        full = lax.dynamic_update_slice_in_dim(full, going_up, (here - far) % ways * hop, axis=dim)
+        if 2 * far < ways:
+            going_down = lax.ppermute(going_down, axis, [(d, (d - 1) % ways) for d in range(ways)])
+            full = lax.dynamic_update_slice_in_dim(
+                full, going_down, (here + far) % ways * hop, axis=dim
+            )
+    return full
 
 
 def positions(doc_rows):
@@ -115,7 +133,7 @@
 
 
 def gather_shard(piece):
-    return lax.all_gather(piece, "shard", axis=0, tiled=True)
+    return collect(piece, "shard", 0)
 
 
 def shards(

time: 1000 us -> 1000 us (level)
  waiting for transfers between devices: 663 us -> 576 us
  starting transfers between devices: 0.33 us -> 51.3 us
  local copies, waits for them, and re-layouts: 60.7 us -> 98.5 us
    all_gather x4 -> x0, waiting for transfers between devices: 251 us -> none  [gather_shard(): return lax.all_gather(piece, 'shard', axis=0, tiled=True)]
    ppermute x0 -> x12, waiting for transfers between devices: none -> 166 us  [the longest x8 147 us: collect(): lax.ppermute(going_up, axis, [(d, (d + 1) % ways) for d in range(ways)])]
    ppermute x0 -> x12, starting transfers between devices: none -> 51.1 us  [the longest x8 37.6 us: collect(): lax.ppermute(going_up, axis, [(d, (d + 1) % ways) for d in range(ways)])]
    dynamic_update_slice x0 -> x15, local copies, waits for them, and re-layouts: none -> 19.1 us  [the longest x8 10.6 us: collect(): lax.dynamic_update_slice_in_dim(full, going_up, (here - far) % ways * hop...]
    unnamed x105 -> x113, local copies, waits for them, and re-layouts: 28 us -> 29.9 us
  transfers between devices with their start and end apart: 8 -> 16, of which waited for: 8 -> 12; matrix products, arithmetic and copies ran while one was open for 12% -> 15% of each run, Pallas kernels for 0% -> 0%
where the time goes in v1:
time: 1000 us; the launch traced here: 994 us
  waiting for transfers between devices  576 us (58%)
  matrix products  203 us (20%)
  local copies, waits for them, and re-layouts  98.5 us (10%)
  starting transfers between devices  51.3 us (5%)
  other arithmetic  51.1 us (5%)
  between operations  14.9 us (1%)
    psum x1, waiting for transfers between devices, shards(): grad_in_own = lax.psum(grad_in_here.astype(bf16), 'rep').astype(f32)  191 us
    ppermute x8, waiting for transfers between devices, collect(): lax.ppermute(going_up, axis, [(d, (d + 1) % ways) for d in range(ways)])  147 us
    reduce_scatter x1, waiting for transfers between devices, reduce_joint(): part = lax.psum_scatter(joint, 'shard', scatter_dimension=0, tiled=True)  76.5 us
    reduce_scatter x1, waiting for transfers between devices, shards(): lax.psum_scatter(combined.astype(bf16), 'shard', scatter_dimension=0, til...  74.4 us
    reduce_scatter x1, waiting for transfers between devices, shards(): lax.psum_scatter(back_rows, 'shard', scatter_dimension=0, tiled=True)  67.9 us
    ppermute x8, starting transfers between devices, collect(): lax.ppermute(going_up, axis, [(d, (d + 1) % ways) for d in range(ways)])  37.6 us
    unnamed x113, local copies, waits for them, and re-layouts  29.9 us
    dot_general x1, matrix products, experts(): jnp.einsum('td,efd->etf', dy_rows, down_w, preferred_element_type=f32)  28.3 us
  transfers between devices with their start and end apart: 16, of which 12 were waited for; matrix products, arithmetic and copies ran while one was open for 15% of the time, Pallas kernels for 0%

profile of v1, /device:TPU:0, one launch (start us, length us, event | category | flops | bytes accessed | tf_op | source)
XLA Modules:
  0.0 994.5 jit_solution(17348019589677428760)
XLA Ops:
  33.7 44.1 %collective-permute-done.3 = bf16[256,1024]{1,0:T(8,128)(2,1)} collective-permute-done((bf16[256,1024]{1,0:T(8,128)(2,1)}, bf16[256,1024]{1,0:T(8,128)(2,1)}, u32[]{:S(2)}, u32[]{:S(2)}) %collective-permute-start.3) | collective-permute-done | bytes 524320 | tf_op jit(solution)/shard_map/ppermute | solution.py:24
  77.8 9.8 collective-permute-start.5
  98.1 27.4 %collective-permute-done.5 = bf16[256,1024]{1,0:T(8,128)(2,1)S(1)} collective-permute-done((bf16[256,1024]{1,0:T(8,128)(2,1)}, bf16[256,1024]{1,0:T(8,128)(2,1)S(1)}, u32[]{:S(2)}, u32[]{:S(2)}) %collective-permute-start.5) | collective-permute-done | bytes 524320 | tf_op jit(solution)/shard_map/ppermute | solution.py:24
  131.9 16.7 %collective-permute-done.2 = bf16[256,2176]{1,0:T(8,128)(2,1)} collective-permute-done((bf16[256,2176]{1,0:T(8,128)(2,1)}, bf16[256,2176]{1,0:T(8,128)(2,1)}, u32[]{:S(2)}, u32[]{:S(2)}) %collective-permute-start.2) | collective-permute-done | bytes 1114144 | tf_op jit(solution)/shard_map/ppermute | solution.py:24
  169.1 9.1 fusion.70
  206.8 20.3 %collective-permute-done.6 = bf16[512,1024]{0,1:T(8,128)(2,1)} collective-permute-done((bf16[512,1024]{0,1:T(8,128)(2,1)S(1)}, bf16[512,1024]{0,1:T(8,128)(2,1)}, u32[]{:S(2)}, u32[]{:S(2)}) %collective-permute-start.6) | collective-permute-done | bytes 1048608 | tf_op jit(solution)/shard_map/ppermute | solution.py:24
  227.1 21.3 %collective-permute-start.8 = (bf16[512,1024]{0,1:T(8,128)(2,1)}, bf16[512,1024]{0,1:T(8,128)(2,1)}, u32[]{:S(2)}, u32[]{:S(2)}) collective-permute-start(bf16[512,1024]{0,1:T(8,128)(2,1)} %collective-permute-done.6), channel_id=1, source_target_pairs={{0,1},{1,2},{2,3},{3,0},{4,5},{5,6},{6,7},{7,4},{8,9},{9,10},{10,1... | collective-permute-start | bytes 3145736 | tf_op jit(solution)/shard_map/ppermute | solution.py:24
  259.5 18.1 %collective-permute-done.11 = bf16[512,1152]{0,1:T(8,128)(2,1)S(1)} collective-permute-done((bf16[512,1152]{0,1:T(8,128)(2,1)}, bf16[512,1152]{0,1:T(8,128)(2,1)S(1)}, u32[]{:S(2)}, u32[]{:S(2)}) %collective-permute-start.11) | collective-permute-done | bytes 1179680 | tf_op jit(solution)/shard_map/ppermute | solution.py:24
  280.2 16.7 %collective-permute-done.7 = bf16[512,1024]{0,1:T(8,128)(2,1)} collective-permute-done((bf16[512,1024]{0,1:T(8,128)(2,1)S(1)}, bf16[512,1024]{0,1:T(8,128)(2,1)}, u32[]{:S(2)}, u32[]{:S(2)}) %collective-permute-start.7) | collective-permute-done | bytes 1048608 | tf_op jit(solution)/shard_map/ppermute | solution.py:27
  300.5 20.4 %collective-permute-done.8 = bf16[512,1024]{0,1:T(8,128)(2,1)} collective-permute-done((bf16[512,1024]{0,1:T(8,128)(2,1)}, bf16[512,1024]{0,1:T(8,128)(2,1)}, u32[]{:S(2)}, u32[]{:S(2)}) %collective-permute-start.8) | collective-permute-done | bytes 1048608 | tf_op jit(solution)/shard_map/ppermute | solution.py:24
  323.5 25.2 %convolution_bitcast_fusion = f32[4,2048,1024]{1,2,0:T(8,128)} fusion(bf16[4,1024,1024]{2,1,0:T(8,128)(2,1)} %param.31, bf16[2048,1024]{1,0:T(8,128)(2,1)} %constant_dynamic-update-slice_fusion.4), kind=kOutput, calls=%fused_computation.2 | convolution fusion | flops 17179869184 | bytes 46137344 | tf_op jit(solution)/shard_map/td,edf->etf/dot_general | solution.py:325
  353.9 28.3 %multiply_convert_fusion.1 = (bf16[4,2048,512]{1,2,0:T(8,128)(2,1)}, bf16[4,2048,512]{1,2,0:T(8,128)(2,1)}, f32[4,2048]{1,0:T(4,128)S(1)}, bf16[4,2048,512]{1,2,0:T(8,128)(2,1)}) fusion(f32[4,2048,1024]{1,2,0:T(8,128)} %convolution_bitcast_fusion, f32[4,2048]{1,0:T(4,128)S(1)} %dynamic-slice_bitcast_fusion, bf16[4,512,1024]{2,1,0:T(8,128)(2,1)} %param.32, ...), kind=kOutput, calls=%fused_computation.15 | convolution fusion | flops 8669618176 | bytes 67174400 | tf_op jit(solution)/shard_map/td,efd->etf/dot_general | solution.py:331
  382.3 23.1 %bitcast_convert_fusion = bf16[2048,1024]{0,1:T(8,128)(2,1)S(1)} fusion(bf16[4,1024,1024]{2,1,0:T(8,128)(2,1)} %param.31, bf16[4,2048,512]{1,2,0:T(8,128)(2,1)} %get-tuple-element.120, bf16[4,2048,512]{1,2,0:T(8,128)(2,1)} %get-tuple-element.119), kind=kOutput, calls=%fused_computation.26 | convolution fusion | flops 17215520768 | bytes 29360128 | tf_op jit(solution)/shard_map/etf,edf->td/dot_general | solution.py:222
  411.9 14.0 %bitcast_convert_fusion.1 = bf16[2048,1024]{0,1:T(8,128)(2,1)} fusion(bf16[4,512,1024]{2,1,0:T(8,128)(2,1)} %param.32, bf16[4,2048,512]{1,2,0:T(8,128)(2,1)} %get-tuple-element.122, f32[4,2048]{1,0:T(4,128)S(1)} %dynamic-slice_bitcast_fusion), kind=kOutput, calls=%fused_computation.27 | convolution fusion | flops 8604614656 | bytes 16809984 | tf_op jit(solution)/shard_map/etf,efd->td/dot_general | solution.py:220
  427.3 67.9 %reduce-scatter.6.cloned.1.call-done = bf16[512,1152]{0,1:T(8,128)(2,1)} async-done(((bf16[2048,1152]{0,1:T(8,128)(2,1)}), bf16[512,1152]{0,1:T(8,128)(2,1)}) %reduce-scatter.6.cloned.1.call-update) | async-done | bytes 1179664 | tf_op jit(solution)/shard_map/reduce_scatter | solution.py:240
  500.4 74.4 %reduce-scatter.4.cloned.1.call-done = bf16[512,1024]{0,1:T(8,128)(2,1)} async-done(((bf16[2048,1024]{0,1:T(8,128)(2,1)}), bf16[512,1024]{0,1:T(8,128)(2,1)}) %reduce-scatter.4.cloned.1.call-update) | async-done | bytes 1048592 | tf_op jit(solution)/shard_map/reduce_scatter | solution.py:221
  585.1 15.1 %fusion.2 = (f32[8,2,512]{2,1,0:T(2,128)S(1)}, f32[8,512,512,2]{2,1,3,0:T(8,128)}) fusion(f32[8,2,512,512]{2,3,1,0:T(8,128)} %get-tuple-element.144, f32[8,2,512]{2,1,0:T(2,128)} %bitcast.139, bf16[512,8,64,1]{0,2,3,1:T(8,128)(2,1)S(1)} %bitcast.128, bf16[512,8,2,64]{0,3,2,1:T(8,128)(2,1)S(1)} %bitcast.120), kind=kOutput, calls=%fused_computation.8 | convolution fusion | flops 549445632 | bytes 35192832 | tf_op jit(solution)/shard_map/qgrd,kgd->grqk/dot_general | solution.py:111
  601.6 8.3 fusion.4
  639.3 10.6 %concatenate.62 = bf16[1024,3200]{1,0:T(8,128)(2,1)} concatenate(bf16[1024,2048]{1,0:T(8,128)(2,1)} %convolution_convert_fusion, bf16[1024,1024]{1,0:T(8,128)(2,1)S(1)} %copy-done.16, bf16[1024,16]{1,0:T(8,128)(2,1)S(1)} %copy.172, bf16[1024,1]{1,0:T(8,128)(2,1)} %convert_element_type.230, bf16[1024,1]{1,0:T(8,128)(2,1)} %convert_element_type.231, bf16[1024,110]{1,0:T(8,128)(2,1)} %broadcast_in_dim.97), dimensions={1} | concatenate | bytes 13107200 | tf_op jit(solution)/shard_map/concatenate | solution.py:286
  650.7 13.9 %fusion.31 = bf16[4,512,1024]{2,1,0:T(8,128)(2,1)} fusion(bf16[2048,1152]{0,1:T(8,128)(2,1)} %constant_dynamic-update-slice_fusion, bf16[4,2048,512]{1,2,0:T(8,128)(2,1)} %get-tuple-element.122, f32[4,2048]{1,0:T(4,128)S(1)} %copy-done.37), kind=kOutput, calls=%fused_computation.50 | convolution fusion | flops 8604614656 | bytes 16809984 | tf_op jit(solution)/shard_map/etf,td->efd/dot_general | solution.py:242
  664.6 24.5 %convert_bitcast_fusion = bf16[4,1024,1024]{1,2,0:T(8,128)(2,1)} fusion(bf16[4,2048,512]{1,2,0:T(8,128)(2,1)} %get-tuple-element.120, bf16[4,2048,512]{1,2,0:T(8,128)(2,1)} %get-tuple-element.119, bf16[2048,1024]{1,0:T(8,128)(2,1)} %constant_dynamic-update-slice_fusion.4), kind=kOutput, calls=%fused_computation.28 | convolution fusion | flops 17217617920 | bytes 29360128 | tf_op jit(solution)/shard_map/td,etf->edf/dot_general | solution.py:241
  689.0 76.5 %reduce-scatter.8.cloned.1.call-done = bf16[256,3200]{1,0:T(8,128)(2,1)} async-done(((bf16[1024,3200]{1,0:T(8,128)(2,1)}), bf16[256,3200]{1,0:T(8,128)(2,1)}) %reduce-scatter.8.cloned.1.call-update) | async-done | bytes 1638416 | tf_op jit(solution)/shard_map/reduce_scatter | solution.py:319
  771.5 191.0 %all-reduce.3.cloned.1.call-done = (bf16[4,1024,1024]{1,2,0:T(8,128)(2,1)}, bf16[256,3200]{1,0:T(8,128)(2,1)}, bf16[4,512,1024]{2,1,0:T(8,128)(2,1)}) async-done(((bf16[4,1024,1024]{1,2,0:T(8,128)(2,1)}, bf16[256,3200]{1,0:T(8,128)(2,1)}, bf16[4,512,1024]{2,1,0:T(8,128)(2,1)}), (bf16[4,1024,1024]{1,2,0:T(8,128)(2,1)}, bf16[256,3200]{1,0:T(8,128)(2,1)}, ...) | async-done | bytes 14221328 | tf_op jit(solution)/shard_map/psum | solution.py:243
  967.1 12.5 %copy.179 = f32[4,1024,1024]{2,1,0:T(8,128)} copy(bf16[4,1024,1024]{1,2,0:T(8,128)(2,1)} %get-tuple-element.112) | data formatting | bytes 25165824
  (242 shorter events, 190.3 us)
Async XLA Ops:
  7.2 488.0 %reduce-scatter.6.cloned.1.call-start = ((), (), s32[]{:S(2)}) async-start(), calls=%async_computation.4 | async-start | bytes 5898240 | tf_op jit(solution)/shard_map/reduce_scatter | solution.py:240
  12.0 78.9 %collective-permute-start = (bf16[256,2176]{1,0:T(8,128)(2,1)S(1)}, bf16[256,2176]{1,0:T(8,128)(2,1)}, u32[]{:S(2)}, u32[]{:S(2)}) collective-permute-start(bf16[256,2176]{1,0:T(8,128)(2,1)S(1)} %concatenate.49), channel_id=1, source_target_pairs={{0,1},{1,2},{2,3},{3,0},{4,5},{5,6},{6,7},{7,4},{8,9},{9,10},{10,1... | collective-permute-start | bytes 3342344 | tf_op jit(solution)/shard_map/ppermute | solution.py:24
  15.1 112.9 %collective-permute-start.1 = (bf16[256,2176]{1,0:T(8,128)(2,1)S(1)}, bf16[256,2176]{1,0:T(8,128)(2,1)}, u32[]{:S(2)}, u32[]{:S(2)}) collective-permute-start(bf16[256,2176]{1,0:T(8,128)(2,1)S(1)} %concatenate.49), channel_id=1, source_target_pairs={{0,3},{1,0},{2,1},{3,2},{4,7},{5,4},{6,5},{7,6},{8,11},{9,8},{10,9... | collective-permute-start | bytes 3342344 | tf_op jit(solution)/shard_map/ppermute | solution.py:27
  17.2 60.6 %collective-permute-start.3 = (bf16[256,1024]{1,0:T(8,128)(2,1)}, bf16[256,1024]{1,0:T(8,128)(2,1)}, u32[]{:S(2)}, u32[]{:S(2)}) collective-permute-start(bf16[256,1024]{1,0:T(8,128)(2,1)} %param.28), channel_id=1, source_target_pairs={{0,1},{1,2},{2,3},{3,0},{4,5},{5,6},{6,7},{7,4},{8,9},{9,10},{10,1... | collective-permute-start | bytes 1572872 | tf_op jit(solution)/shard_map/ppermute | solution.py:24
  17.2 79.0 %collective-permute-start.4 = (bf16[256,1024]{1,0:T(8,128)(2,1)}, bf16[256,1024]{1,0:T(8,128)(2,1)}, u32[]{:S(2)}, u32[]{:S(2)}) collective-permute-start(bf16[256,1024]{1,0:T(8,128)(2,1)} %param.28), channel_id=1, source_target_pairs={{0,3},{1,0},{2,1},{3,2},{4,7},{5,4},{6,5},{7,6},{8,11},{9,8},{10,9... | collective-permute-start | bytes 1572872 | tf_op jit(solution)/shard_map/ppermute | solution.py:27
  27.3 175.7 %collective-permute-start.9 = (bf16[512,1152]{0,1:T(8,128)(2,1)}, bf16[512,1152]{0,1:T(8,128)(2,1)}, u32[]{:S(2)}, u32[]{:S(2)}) collective-permute-start(bf16[512,1152]{0,1:T(8,128)(2,1)} %get-tuple-element.139), channel_id=1, source_target_pairs={{0,1},{1,2},{2,3},{3,0},{4,5},{5,6},{6,7},{7,4},{8,9},{9,10},{10,1... | collective-permute-start | bytes 3538952 | tf_op jit(solution)/shard_map/ppermute | solution.py:24
  33.1 161.0 %copy-start.6 = (bf16[512,1024]{0,1:T(8,128)(2,1)}, bf16[512,1024]{0,1:T(8,128)(2,1)S(1)}, u32[]{:S(2)}) copy-start(bf16[512,1024]{0,1:T(8,128)(2,1)S(1)} %copy.140) | copy-start | bytes 3145732
  33.4 132.8 %copy-start.17 = (f32[512,32]{0,1:T(8,128)}, f32[512,32]{0,1:T(8,128)S(1)}, u32[]{:S(2)}) copy-start(f32[512,32]{0,1:T(8,128)S(1)} %get-tuple-element.141) | copy-start | bytes 196612
  33.4 132.8 %copy-start.19 = (f32[512,32]{0,1:T(8,128)}, f32[512,32]{0,1:T(8,128)S(1)}, u32[]{:S(2)}) copy-start(f32[512,32]{0,1:T(8,128)S(1)} %get-tuple-element.142) | copy-start | bytes 196612
  33.7 118.5 %copy-start.43 = (f32[512]{0:T(512)}, f32[512]{0:T(512)S(1)}, u32[]{:S(2)}) copy-start(f32[512]{0:T(512)S(1)} %add_rsqrt_fusion.1) | copy-start | bytes 6148
  77.8 47.6 %collective-permute-start.5 = (bf16[256,1024]{1,0:T(8,128)(2,1)}, bf16[256,1024]{1,0:T(8,128)(2,1)S(1)}, u32[]{:S(2)}, u32[]{:S(2)}) collective-permute-start(bf16[256,1024]{1,0:T(8,128)(2,1)} %collective-permute-done.3), channel_id=1, source_target_pairs={{0,1},{1,2},{2,3},{3,0},{4,5},{5,6},{6,7},{7,4},{8,9},{9,10},{10,1... | collective-permute-start | bytes 1572872 | tf_op jit(solution)/shard_map/ppermute | solution.py:24
  90.9 57.7 %collective-permute-start.2 = (bf16[256,2176]{1,0:T(8,128)(2,1)}, bf16[256,2176]{1,0:T(8,128)(2,1)}, u32[]{:S(2)}, u32[]{:S(2)}) collective-permute-start(bf16[256,2176]{1,0:T(8,128)(2,1)} %collective-permute-done), channel_id=1, source_target_pairs={{0,1},{1,2},{2,3},{3,0},{4,5},{5,6},{6,7},{7,4},{8,9},{9,10},{10,1... | collective-permute-start | bytes 3342344 | tf_op jit(solution)/shard_map/ppermute | solution.py:24
  199.1 28.1 %collective-permute-start.6 = (bf16[512,1024]{0,1:T(8,128)(2,1)S(1)}, bf16[512,1024]{0,1:T(8,128)(2,1)}, u32[]{:S(2)}, u32[]{:S(2)}) collective-permute-start(bf16[512,1024]{0,1:T(8,128)(2,1)S(1)} %multiply_convert_fusion.3), channel_id=1, source_target_pairs={{0,1},{1,2},{2,3},{3,0},{4,5},{5,6},{6,7},{7,4},{8,9},{9,10},{10,1... | collective-permute-start | bytes 3145736 | tf_op jit(solution)/shard_map/ppermute | solution.py:24
  199.1 53.6 %collective-permute-start.10 = (bf16[512,1152]{0,1:T(8,128)(2,1)}, bf16[512,1152]{0,1:T(8,128)(2,1)}, u32[]{:S(2)}, u32[]{:S(2)}) collective-permute-start(bf16[512,1152]{0,1:T(8,128)(2,1)} %get-tuple-element.139), channel_id=1, source_target_pairs={{0,3},{1,0},{2,1},{3,2},{4,7},{5,4},{6,5},{7,6},{8,11},{9,8},{10,9... | collective-permute-start | bytes 3538952 | tf_op jit(solution)/shard_map/ppermute | solution.py:27
  202.9 74.7 %collective-permute-start.11 = (bf16[512,1152]{0,1:T(8,128)(2,1)}, bf16[512,1152]{0,1:T(8,128)(2,1)S(1)}, u32[]{:S(2)}, u32[]{:S(2)}) collective-permute-start(bf16[512,1152]{0,1:T(8,128)(2,1)} %collective-permute-done.9), channel_id=1, source_target_pairs={{0,1},{1,2},{2,3},{3,0},{4,5},{5,6},{6,7},{7,4},{8,9},{9,10},{10,1... | collective-permute-start | bytes 3538952 | tf_op jit(solution)/shard_map/ppermute | solution.py:24
  202.9 94.0 %collective-permute-start.7 = (bf16[512,1024]{0,1:T(8,128)(2,1)S(1)}, bf16[512,1024]{0,1:T(8,128)(2,1)}, u32[]{:S(2)}, u32[]{:S(2)}) collective-permute-start(bf16[512,1024]{0,1:T(8,128)(2,1)S(1)} %multiply_convert_fusion.3), channel_id=1, source_target_pairs={{0,3},{1,0},{2,1},{3,2},{4,7},{5,4},{6,5},{7,6},{8,11},{9,8},{10,9... | collective-permute-start | bytes 3145736 | tf_op jit(solution)/shard_map/ppermute | solution.py:27
  227.1 93.8 %collective-permute-start.8 = (bf16[512,1024]{0,1:T(8,128)(2,1)}, bf16[512,1024]{0,1:T(8,128)(2,1)}, u32[]{:S(2)}, u32[]{:S(2)}) collective-permute-start(bf16[512,1024]{0,1:T(8,128)(2,1)} %collective-permute-done.6), channel_id=1, source_target_pairs={{0,1},{1,2},{2,3},{3,0},{4,5},{5,6},{6,7},{7,4},{8,9},{9,10},{10,1... | collective-permute-start | bytes 3145736 | tf_op jit(solution)/shard_map/ppermute | solution.py:24
  411.8 163.0 %reduce-scatter.4.cloned.1.call-start = ((), (), s32[]{:S(2)}) async-start(), calls=%async_computation.3 | async-start | bytes 5242880 | tf_op jit(solution)/shard_map/reduce_scatter | solution.py:221
  425.9 70.1 %copy-start.2 = (f32[512,1024]{0,1:T(8,128)S(1)}, f32[512,1024]{0,1:T(8,128)}, u32[]{:S(2)}) copy-start(f32[512,1024]{0,1:T(8,128)} %copy-done.1) | copy-start | bytes 6291460
  425.9 70.1 %copy-start.34 = (f32[1024,1]{0,1:T(1,128)S(1)}, f32[1024,1]{0,1:T(1,128)}, u32[]{:S(2)}) copy-start(f32[1024,1]{0,1:T(1,128)} %copy-done.33) | copy-start | bytes 12292
  425.9 70.1 %copy-start.39 = (f32[512]{0:T(512)S(1)}, f32[512]{0:T(512)}, u32[]{:S(2)}) copy-start(f32[512]{0:T(512)} %copy-done.38) | copy-start | bytes 6148
  425.9 73.5 %copy-start.5 = (bf16[512,1024]{0,1:T(8,128)(2,1)S(1)}, bf16[512,1024]{0,1:T(8,128)(2,1)}, u32[]{:S(2)}) copy-start(bf16[512,1024]{0,1:T(8,128)(2,1)} %copy-done.4) | copy-start | bytes 3145732
  425.9 339.6 %reduce-scatter.8.cloned.1.call-start = ((), (), s32[]{:S(2)}) async-start(), calls=%async_computation.5 | async-start | bytes 8192000 | tf_op jit(solution)/shard_map/reduce_scatter | solution.py:319
  649.9 312.5 %all-reduce.3.cloned.1.call-start = ((), (), s32[]{:S(2)}) async-start(), calls=%async_computation.6 | async-start | bytes 28442624 | tf_op jit(solution)/shard_map/psum | solution.py:243
  (45 other events, 486.7 us)
Sparse Core Ops, SparseCore 0:
  411.9 83.2 reduce-scatter.5
  497.5 77.2 reduce-scatter.3
  650.0 115.4 reduce-scatter.7
  770.6 191.8 all-reduce.2
